TPU v7x, 128 devices: a whole 4x4x4 slice. The times are simulated.
128 devices in a mesh: rows: 32 (over y, x_lo, z), cols: 4 (over x_hi, core).
Axes of the slice: x: 4 (x_hi: 2, x_lo: 2; x = x_hi * 2 + x_lo), y: 4, z: 4, core: 2. Of those that a mesh axis runs over, the one named last changes fastest.
Arguments:
- local_tiles: bfloat16 [1024, 24, 64, 64], P('rows'), may hold values from -0.109375 to 0.109375
- local_cols: int32 [1024, 24], P('rows'), may hold values from 0 to 31, as said below
- section_tiles: bfloat16 [1024, 2, 12, 64, 64], P('rows'), may hold values from -0.109375 to 0.109375
- section_cols: int32 [1024, 2, 12], P('rows'), may hold values from 0 to 31, as said below
- owners: int32 [2], replicated, may hold values from 0 to 31
- prol_tiles: bfloat16 [1024, 8, 64, 64], P('rows', 'cols'), may hold values from -6 to 6
- prol_cols: int32 [1024, 8], P('rows', 'cols'), may hold values from 0 to 7, as said below
Outputs:
- product: bfloat16 [65536, 2048], P('rows')
Inputs may be any that keep to these rules, and one draw needn't show every extreme that they name: `local_cols`: the 24 entries of one block row are distinct. `section_cols`: the 12 entries of one block row and section are distinct. `prol_cols`: within one block row, the 2 entries of each index of cols are distinct.
All inputs are finite; a program needn't handle non-finite values.
Results may differ from a plain program's by a relative error of at most 0.001.
Values may be sent and summed in bfloat16 or wider, within the bound.
A program may use at most 256 MiB of HBM per device.

v0:
```python
import jax
import jax.numpy as jnp
from jax import lax
from jax.sharding import PartitionSpec as P

CTD = 8
KPD = 2


def broadcast(array, axis, root):
    mine = lax.axis_index(axis) == root
    return lax.psum(jnp.where(mine, array, jnp.zeros_like(array)), axis)


def densify_prolong(tiles, tile_cols):
    count = tiles.shape[0]
    slots = tiles.shape[1]
    width = tiles.shape[-1]
    tile_total = slots // KPD * CTD
    offsets = jnp.arange(slots) // KPD * CTD
    target = tile_cols + offsets[None, :]
    onehot = (target[:, :, None] == jnp.arange(tile_total, dtype=jnp.int32)[None, None, :]).astype(
        jnp.bfloat16
    )
    dense = jnp.einsum("rjt,rjab->ratb", onehot, tiles, preferred_element_type=jnp.float32)
    return dense.astype(jnp.bfloat16).reshape(count * width, tile_total * width)


def densify_stiff(tiles, tile_cols, count):
    width = tiles.shape[-1]
    onehot = (tile_cols[:, :, None] == jnp.arange(count, dtype=jnp.int32)[None, None, :]).astype(
        jnp.bfloat16
    )
    dense = jnp.einsum("ikr,ikab->iarb", onehot, tiles, preferred_element_type=jnp.float32)
    return dense.astype(jnp.bfloat16).reshape(tiles.shape[0] * width, count * width)


def per_device(local_tiles, local_cols, section_tiles, section_cols, owners, prol_tiles, prol_cols):
    count = local_tiles.shape[0]
    tiles, tile_cols = (prol_tiles, prol_cols)
    source = densify_prolong(tiles, tile_cols)
    total = jnp.dot(
        densify_stiff(local_tiles, local_cols, count), source, preferred_element_type=jnp.float32
    )
    for section in range(owners.shape[0]):
        panel = broadcast(source, "rows", owners[section])
        section_dense = densify_stiff(section_tiles[:, section], section_cols[:, section], count)
        total = total + jnp.dot(section_dense, panel, preferred_element_type=jnp.float32)
    result = total.astype(jnp.bfloat16)
    result = lax.all_gather(result, "cols", axis=1, tiled=True)
    return result


def solution(mesh):
    in_specs = (
        P("rows", None, None, None),
        P("rows", None),
        P("rows", None, None, None, None),
        P("rows", None, None),
        P(),
        P("rows", "cols", None, None),
        P("rows", "cols"),
    )
    out_specs = P("rows", None)
    return jax.shard_map(
        per_device, mesh=mesh, in_specs=in_specs, out_specs=out_specs, check_vma=False
    )
```

profile of v0, /device:TPU:1, one launch (start us, length us, event | category | flops | bytes accessed | tf_op | source)
XLA Modules:
  0.0 437.7 jit_solution(5459273139037373132)
XLA Ops:
  6.5 0.0 copy-start
  6.5 0.0 all-reduce.3.cloned.1.call-start
  6.6 0.8 broadcast_add_fusion
  7.4 0.1 copy.18
  7.5 0.3 copy-done
  7.8 3.2 convert_bitcast_fusion.3
  11.0 5.4 %reshape.31 = bf16[2048,512]{1,0:T(8,128)(2,1)S(1)} reshape(bf16[32,64,8,64]{3,2,1,0:T(8,128)(2,1)} %convert_bitcast_fusion.3) | data formatting | bytes 4194304 | tf_op jit(solution)/shard_map/reshape | solution.py:26
  16.4 0.0 copy-start.3
  16.4 0.0 copy-done.5
  16.4 0.6 fusion.21
  18.2 2.2 broadcast_select_fusion
  20.4 0.0 all-reduce.3.cloned.1.call-update
  20.5 0.2 all-gather.2.cloned.1.call-start
  20.7 0.1 copy.16
  20.8 18.3 %convert_bitcast_fusion.2 = bf16[32,64,32,64]{3,2,1,0:T(8,128)(2,1)} fusion(bf16[32,24,64,64]{3,2,1,0:T(8,128)(2,1)} %param.7, s32[32,24]{1,0:T(8,128)S(1)} %copy.16), kind=kOutput, calls=%fused_computation.2 | convolution fusion | flops 205545472 | bytes 14683136 | tf_op jit(solution)/shard_map/ikr,ikab->iarb/dot_general | solution.py:34
  39.1 23.5 %reshape.30 = bf16[2048,2048]{1,0:T(8,128)(2,1)} reshape(bf16[32,64,32,64]{3,2,1,0:T(8,128)(2,1)} %convert_bitcast_fusion.2) | data formatting | bytes 16777216 | tf_op jit(solution)/shard_map/reshape | solution.py:35
  62.6 12.9 %fusion.19 = (bf16[32,1,12,64,64]{4,3,2,1,0:T(8,128)(2,1)}, bf16[32,1,12,64,64]{4,3,2,1,0:T(8,128)(2,1)}) fusion(bf16[32,2,12,64,64]{4,3,2,1,0:T(8,128)(2,1)} %param.9), kind=kLoop, calls=%fused_computation.31 | loop fusion | bytes 12582912 | tf_op jit(solution)/shard_map/slice | solution.py:47
  75.5 0.1 copy.34
  75.5 11.6 %convert_bitcast_fusion.1 = bf16[32,64,32,64]{3,2,1,0:T(8,128)(2,1)} fusion(bf16[32,1,12,64,64]{4,3,2,1,0:T(8,128)(2,1)} %get-tuple-element.8, s32[32,12]{1,0:T(8,128)S(1)} %bitcast.55), kind=kOutput, calls=%fused_computation.1 | convolution fusion | flops 104869888 | bytes 11535872 | tf_op jit(solution)/shard_map/ikr,ikab->iarb/dot_general | solution.py:34
  87.2 23.5 %reshape.32 = bf16[2048,2048]{1,0:T(8,128)(2,1)} reshape(bf16[32,64,32,64]{3,2,1,0:T(8,128)(2,1)} %convert_bitcast_fusion.1) | data formatting | bytes 16777216 | tf_op jit(solution)/shard_map/reshape | solution.py:35
  110.6 0.1 copy.35
  110.7 11.8 %convert_bitcast_fusion = bf16[32,64,32,64]{3,2,1,0:T(8,128)(2,1)} fusion(bf16[32,1,12,64,64]{4,3,2,1,0:T(8,128)(2,1)} %get-tuple-element.7, s32[32,12]{1,0:T(8,128)S(1)} %bitcast.54), kind=kOutput, calls=%fused_computation | convolution fusion | flops 104869888 | bytes 11535872 | tf_op jit(solution)/shard_map/ikr,ikab->iarb/dot_general | solution.py:34
  122.5 23.5 %reshape.33 = bf16[2048,2048]{1,0:T(8,128)(2,1)} reshape(bf16[32,64,32,64]{3,2,1,0:T(8,128)(2,1)} %convert_bitcast_fusion) | data formatting | bytes 16777216 | tf_op jit(solution)/shard_map/reshape | solution.py:35
  146.0 9.5 %fusion.22 = f32[2048,512]{1,0:T(8,128)} fusion(bf16[2048,2048]{1,0:T(8,128)(2,1)} %reshape.30, bf16[2048,512]{1,0:T(8,128)(2,1)S(1)} %reshape.31), kind=kOutput, calls=%fused_computation.34 | convolution fusion | flops 4294967296 | bytes 14680064 | tf_op jit(solution)/shard_map/dot_general | solution.py:42
  155.5 168.9 %all-reduce.3.cloned.1.call-done = (bf16[2048,512]{1,0:T(8,128)(2,1)}, bf16[2048,512]{1,0:T(8,128)(2,1)}) async-done(((bf16[2048,512]{1,0:T(8,128)(2,1)}, bf16[2048,512]{1,0:T(8,128)(2,1)}), (bf16[2048,512]{1,0:T(8,128)(2,1)}, bf16[2048,512]{1,0:T(8,128)(2,1)})) %all-reduce.3.cloned.1.call-update) | async-done | bytes 4194320 | tf_op jit(solution)/shard_map/psum | solution.py:12
  324.4 7.7 %fusion.23 = f32[2048,512]{1,0:T(8,128)S(1)} fusion(bf16[2048,2048]{1,0:T(8,128)(2,1)} %reshape.32, bf16[2048,512]{1,0:T(8,128)(2,1)} %get-tuple-element.5), kind=kOutput, calls=%fused_computation.35 | convolution fusion | flops 4294967296 | bytes 14680064 | tf_op jit(solution)/shard_map/dot_general | solution.py:48
  332.1 0.5 copy-done.7
  332.6 5.6 %add_convert_fusion = bf16[2048,512]{1,0:T(8,128)(2,1)} fusion(f32[2048,512]{1,0:T(8,128)S(1)} %copy-done.7, f32[2048,512]{1,0:T(8,128)S(1)} %fusion.23, bf16[2048,2048]{1,0:T(8,128)(2,1)S(1)} %copy-done.2, bf16[2048,512]{1,0:T(8,128)(2,1)S(1)} %copy-done.6), kind=kOutput, calls=%fused_computation.7 | convolution fusion | flops 4298113024 | bytes 20971520 | tf_op jit(solution)/shard_map/dot_general | solution.py:48
  338.2 0.0 all-gather.2.cloned.1.call-update
  338.3 0.0 copy-start.1
  338.3 84.2 %all-gather.2.cloned.1.call-done = bf16[2048,2048]{1,0:T(8,128)(2,1)} async-done(((bf16[2048,512]{1,0:T(8,128)(2,1)}), bf16[2048,2048]{1,0:T(8,128)(2,1)}) %all-gather.2.cloned.1.call-update) | async-done | bytes 8388624 | tf_op jit(solution)/shard_map/all_gather | solution.py:50
  422.4 8.4 %copy.49 = bf16[2048,2048]{1,0:T(8,128)(2,1)} copy(bf16[2048,2048]{1,0:T(8,128)(2,1)} %all-gather.2.cloned.1.call-done) | data formatting | bytes 16777216
  (12 shorter events, 0.0 us)
Async XLA Ops:
  6.5 1.2 copy-start
  6.5 9.9 %copy-start.5 = (s32[2]{0:T(128)S(1)}, s32[2]{0:T(128)}, u32[]{:S(2)}) copy-start(s32[2]{0:T(128)} %param.11) | copy-start | bytes 28
  6.5 317.8 %all-reduce.3.cloned.1.call-start = ((), (), s32[]{:S(2)}) async-start(), calls=%async_computation.1 | async-start | bytes 8388608 | tf_op jit(solution)/shard_map/psum | solution.py:12
  16.4 4.3 copy-start.3
  20.5 402.0 %all-gather.2.cloned.1.call-start = ((), (), s32[]{:S(2)}) async-start(), calls=%async_computation | async-start | bytes 10485760 | tf_op jit(solution)/shard_map/all_gather | solution.py:50
  62.6 12.9 %copy-start.4 = (s32[32,2,12]{0,1,2:T(2,128)S(1)}, s32[32,2,12]{0,1,2:T(2,128)}, u32[]{:S(2)}) copy-start(s32[32,2,12]{0,1,2:T(2,128)} %param.10) | copy-start | bytes 9220
  324.4 7.7 %copy-start.2 = (bf16[2048,2048]{1,0:T(8,128)(2,1)S(1)}, bf16[2048,2048]{1,0:T(8,128)(2,1)}, u32[]{:S(2)}) copy-start(bf16[2048,2048]{1,0:T(8,128)(2,1)} %reshape.33) | copy-start | bytes 25165828
  324.4 7.7 %copy-start.6 = (bf16[2048,512]{1,0:T(8,128)(2,1)S(1)}, bf16[2048,512]{1,0:T(8,128)(2,1)}, u32[]{:S(2)}) copy-start(bf16[2048,512]{1,0:T(8,128)(2,1)} %get-tuple-element.6) | copy-start | bytes 6291460
  324.4 8.2 %copy-start.7 = (f32[2048,512]{1,0:T(8,128)S(1)}, f32[2048,512]{1,0:T(8,128)}, u32[]{:S(2)}) copy-start(f32[2048,512]{1,0:T(8,128)} %fusion.22) | copy-start | bytes 12582916
  338.3 92.6 %copy-start.1 = (bf16[32,2,64,64]{3,2,1,0:T(8,128)(2,1)S(1)}, bf16[32,2,64,64]{3,2,1,0:T(8,128)(2,1)}, u32[]{:S(2)}) copy-start(bf16[32,2,64,64]{3,2,1,0:T(8,128)(2,1)} %param.12) | copy-start | bytes 1572868
Sparse Core Ops, SparseCore 0:
  20.6 303.7 all-reduce.2
  338.4 84.0 all-gather.1
where the time goes:
time: 440 us; the launch traced here: 438 us
  waiting for transfers between devices  253 us (58%)
  local copies, waits for them, and re-layouts  98.9 us (22%)
  matrix products  67.7 us (15%)
  between operations  14.7 us (3%)
    psum x1, waiting for transfers between devices, broadcast(): return lax.psum(jnp.where(mine, array, jnp.zeros_like(array)), axis)  169 us
    all_gather x1, waiting for transfers between devices, per_device(): result = lax.all_gather(result, 'cols', axis=1, tiled=True)  84.2 us
    reshape x3, local copies, waits for them, and re-layouts, densify_stiff(): dense.astype(jnp.bfloat16).reshape(tiles.shape[0] * width, count * width)  70.4 us
    dot_general x3, matrix products, densify_stiff(): jnp.einsum('ikr,ikab->iarb', onehot, tiles, preferred_element_type=jnp.fl...  41.7 us
    dot_general x2, matrix products, per_device(): jnp.dot(section_dense, panel, preferred_element_type=jnp.float32)  13.3 us
    slice x1, local copies, waits for them, and re-layouts, per_device(): section_tiles[:, section]  12.9 us
    dot_general x1, matrix products, per_device(): jnp.dot(densify_stiff(local_tiles, local_cols, count), source, preferred_...  9.51 us
    unnamed x18, local copies, waits for them, and re-layouts  9.36 us
  transfers between devices with their start and end apart: 2, of which 2 were waited for; matrix products, arithmetic and copies ran while one was open for 31% of the time, Pallas kernels for 0%

commit v1 on v0

v1 whole, which is shorter than its diff:
```python
import jax
import jax.numpy as jnp
from jax import lax
from jax.experimental import pallas as pl
from jax.experimental.pallas import tpu as pltpu
from jax.sharding import PartitionSpec as P

MESH = pl.DeviceIdType.MESH
BF = jnp.bfloat16
F32 = jnp.float32
T = 64
RB = 32
MT = 256
ROWS = RB * T
HALF = 512
WIDE = 2 * HALF
GROUPS = 2


def kernel(
    table, meta, p_hbm, l_hbm, s_hbm, out,
    praw, aloc, asec, pc, pp, mp, r1a, r1b, r1m, s1, s1m, r2, r2m, s2, s2m, rx, rxm, qc, qm, mf,
    d0, d1, dense, ab0, ab1, acc,
    load_sem, send_sem, recv_sem, osend, orecv, olocal,
):
    r = lax.axis_index("rows")
    c = lax.axis_index("cols")
    y, xl, z = r // 8, (r // 4) % 2, r % 4
    xh, core = c // 2, c % 2
    x = xh * 2 + xl

    def y_peer(j):
        return (((y + j) % 4 * 2 + xl) * 4 + z, c)

    def z_peer(j):
        return ((y * 2 + xl) * 4 + (z + j) % 4, c)

    def x_peer(j):
        q = (x + j) % 4
        return ((y * 2 + q % 2) * 4 + z, (q // 2) * 2 + core)

    core_peer = (r, xh * 2 + 1 - core)

    loads = [
        pltpu.make_async_copy(p_hbm, praw, load_sem.at[0]),
        pltpu.make_async_copy(l_hbm, aloc.at[pl.ds(0, 768)], load_sem.at[1]),
        pltpu.make_async_copy(s_hbm, asec.at[pl.ds(0, 768)], load_sem.at[2]),
    ]
    for load in loads:
        load.start()

    barrier = pltpu.get_barrier_semaphore()
    for peer in [f(j) for f in (y_peer, z_peer, x_peer) for j in (1, 2, 3)] + [core_peer]:
        pl.semaphore_signal(barrier, inc=1, device_id=peer, device_id_type=MESH)

    aloc[768] = jnp.zeros((T, T), BF)
    asec[768] = jnp.zeros((T, T), BF)

    loads[0].wait()

    def compact(k, _):
        rows = pl.ds(pl.multiple_of(k * T, T), T)
        pc[rows, :] = jnp.concatenate([praw[2 * k], praw[2 * k + 1]], axis=1)
        return 0

    lax.fori_loop(0, RB, compact, 0)

    def owner(s):
        o = table[3072 + s]
        return o // 8, (o // 4) % 2, o % 4

    sent = []

    def remote(src, dst, peer):
        i = len(sent)
        copy = pltpu.make_async_remote_copy(
            src_ref=src, dst_ref=dst, send_sem=send_sem.at[i], recv_sem=recv_sem.at[i],
            device_id=peer, device_id_type=MESH,
        )
        copy.start()
        sent.append(copy)
        return copy

    def rows_at(base, index, size):
        return pl.ds(pl.multiple_of(base + index * size, size), size)

    pl.semaphore_wait(barrier, 10)

    stage1 = []
    for j in (1, 2, 3):
        stage1.append(remote(pc.at[rows_at(0, (y + j) % 4, 256)], r1a.at[j], y_peer(j)))
        stage1.append(remote(pc.at[rows_at(1024, (z + j) % 4, 256)], r1b.at[j], z_peer(j)))
        stage1.append(remote(meta, r1m.at[j], y_peer(j)))
    partner = [remote(pc, pp, x_peer(2)), remote(meta, mp, x_peer(2))]
    r1a[0] = pc[rows_at(0, y, 256)]
    r1b[0] = pc[rows_at(1024, z, 256)]
    r1m[0] = meta[...]

    stage2, stage3, stage4, stage5 = [], [], [[], []], [[], []]

    def step1():
        for copy in stage1:
            copy.wait_recv()
        for s in range(GROUPS):
            oy, ox, oz = owner(s)
            s1[s, 0] = r1a[(y + 4 - oy) % 4]
            s1[s, 1] = r1b[(z + 4 - oz) % 4]
            s1m[s] = r1m[(y + 4 - oy) % 4]
        for s in range(GROUPS):
            for j in (1, 2, 3):
                stage2.append(remote(s1.at[s, 0, rows_at(0, (z + j) % 4, T)], r2.at[s, 0, j], z_peer(j)))
                stage2.append(remote(s1.at[s, 1, rows_at(0, (y + j) % 4, T)], r2.at[s, 1, j], y_peer(j)))
        for j in (1, 2, 3):
            stage2.append(remote(s1m, r2m.at[j], z_peer(j)))
        for s in range(GROUPS):
            r2[s, 0, 0] = s1[s, 0, rows_at(0, z, T)]
            r2[s, 1, 0] = s1[s, 1, rows_at(0, y, T)]
        r2m[0] = s1m[...]

    def step2():
        for copy in stage2:
            copy.wait_recv()
        for s in range(GROUPS):
            oy, ox, oz = owner(s)
            s2[s, 0] = r2[s, 0, (z + 4 - oz) % 4]
            s2[s, 1] = r2[s, 1, (y + 4 - oy) % 4]
            s2m[s] = r2m[(z + 4 - oz) % 4, s]
        for s in range(GROUPS):
            for j in (1, 2, 3):
                stage3.append(remote(s2.at[s], rx.at[s, j], x_peer(j)))
        for j in (1, 2, 3):
            stage3.append(remote(s2m, rxm.at[j], x_peer(j)))
        for s in range(GROUPS):
            rx[s, 0] = s2[s]
        rxm[0] = s2m[...]

    def step3():
        for copy in stage3:
            copy.wait_recv()
        for s in range(GROUPS):
            oy, ox, oz = owner(s)
            for h in range(2):
                slot = (x + 4 - (h * 2 + ox)) % 4
                qc[s, h, rows_at(0, y * 4 + z, T)] = rx[s, slot, 0]
                qc[s, h, rows_at(1024, z * 4 + y, T)] = rx[s, slot, 1]
                qm[s, h] = rxm[slot, s]
        for s in range(GROUPS):
            for j in (1, 2, 3):
                first = qc.at[s, :, rows_at(0, y * 4 + z, T)]
                second = qc.at[s, :, rows_at(1024, z * 4 + y, T)]
                stage4[s].append(remote(first, first, z_peer(j)))
                stage4[s].append(remote(second, second, y_peer(j)))

    def step4(s):
        for copy in stage4[s]:
            copy.wait_recv()
        for j in (1, 2, 3):
            first = qc.at[s, :, rows_at(0, y, 256)]
            second = qc.at[s, :, rows_at(1024, z, 256)]
            stage5[s].append(remote(first, first, y_peer(j)))
            stage5[s].append(remote(second, second, z_peer(j)))

    def step5(s):
        for copy in stage5[s]:
            copy.wait_recv()

    def spread(src, cols, dst, h):
        mf[...] = cols.astype(F32)
        lane = lax.broadcasted_iota(jnp.int32, (16, 128), 1)
        side = (lane >= T).astype(F32)

        def body(k, _):
            row = jnp.broadcast_to(mf[pl.ds(k, 1), :], (16, 128))
            swapped = jnp.concatenate([row[:, T:], row[:, :T]], axis=1)
            masks = [
                (jnp.where(row == side + 2.0 * p, 1.0, 0.0).astype(BF),
                 jnp.where(swapped == side + 2.0 * p, 1.0, 0.0).astype(BF))
                for p in range(4)
            ]
            for q in range(4):
                rows = pl.ds(pl.multiple_of(k * T + q * 16, 16), 16)
                t = src(rows)
                u = jnp.concatenate([t[:, T:], t[:, :T]], axis=1)
                for p in range(4):
                    dst[rows, h * HALF + p * 128 : h * HALF + (p + 1) * 128] = t * masks[p][0] + u * masks[p][1]
            return 0

        lax.fori_loop(0, RB, body, 0)

    def fill(src, which, m, stores):
        for b in range(4):
            base = which * 1024 + (m * 4 + b) * RB
            for p in range(16):
                pair = jnp.concatenate([src[table[base + 2 * p]], src[table[base + 2 * p + 1]]], axis=1)
                for ref, start in stores:
                    ref[pl.ds(start + b * T, T), p * 128 : (p + 1) * 128] = pair

    def rows_of(m):
        return pl.ds(pl.multiple_of(m * MT, MT), MT)

    spread(lambda rows: pc[rows, :], meta[...], d0, 0)
    loads[1].wait()

    def pass1(m, ab):
        for n in range(2):
            cols = slice(n * 256, (n + 1) * 256)
            acc[rows_of(m), cols] = jnp.dot(ab[...], d0[:, cols], preferred_element_type=F32)

    def start_of(m):
        return pl.multiple_of(m * MT, MT)

    fill(aloc, 0, 0, [(ab0, 0), (dense, 0)])

    def loop1(jj, _):
        m = 2 * jj
        fill(aloc, 0, m + 1, [(ab1, 0), (dense, start_of(m + 1))])
        pass1(m, ab0)
        after = jnp.minimum(m + 2, 7)
        fill(aloc, 0, after, [(ab0, 0), (dense, start_of(after))])
        pass1(m + 1, ab1)
        return 0

    lax.fori_loop(0, 1, loop1, 0)
    step1()
    lax.fori_loop(1, 2, loop1, 0)
    step2()
    lax.fori_loop(2, 3, loop1, 0)
    step3()
    lax.fori_loop(3, 4, loop1, 0)
    step4(0)
    step4(1)

    for copy in partner:
        copy.wait_recv()
    spread(lambda rows: pp[rows, :], mp[...], d0, 1)

    def loop2(m, _):
        for n in range(2, 4):
            cols = slice(n * 256, (n + 1) * 256)
            acc[rows_of(m), cols] = jnp.dot(dense[rows_of(m), :], d0[:, cols], preferred_element_type=F32)
        return 0

    lax.fori_loop(0, 8, loop2, 0)

    loads[2].wait()
    fill(asec, 1, 0, [(ab0, 0)])
    step5(0)
    for h in range(2):
        side = xh * (1 - h) + (1 - xh) * h
        spread(lambda rows: qc[0, side, rows, :], qm[0, side], d1, h)

    def pass3(m, ab):
        for n in range(4):
            cols = slice(n * 256, (n + 1) * 256)
            acc[rows_of(m), cols] += jnp.dot(ab[...], d1[:, cols], preferred_element_type=F32)

    def loop3(jj, _):
        m = 2 * jj
        fill(asec, 1, m + 1, [(ab1, 0)])
        pass3(m, ab0)
        fill(asec, 1, jnp.minimum(m + 2, 7), [(ab0, 0)])
        pass3(m + 1, ab1)
        return 0

    lax.fori_loop(0, 4, loop3, 0)

    fill(asec, 2, 0, [(ab0, 0)])
    step5(1)
    for h in range(2):
        side = xh * (1 - h) + (1 - xh) * h
        spread(lambda rows: qc[1, side, rows, :], qm[1, side], d0, h)

    def results(m):
        copies = []
        for h in range(2):
            side = xh * (1 - h) + (1 - xh) * h
            src = dense.at[rows_of(m), pl.ds(h * HALF, HALF)]
            dst = out.at[rows_of(m), pl.ds(pl.multiple_of((side * 2 + core) * HALF, HALF), HALF)]
            copies.append((
                pltpu.make_async_copy(src, dst, olocal.at[m, h]),
                pltpu.make_async_remote_copy(
                    src_ref=src, dst_ref=dst, send_sem=osend.at[m, h], recv_sem=orecv.at[m, h],
                    device_id=core_peer, device_id_type=MESH,
                ),
            ))
        return copies

    def pass4(m, ab):
        for n in range(4):
            cols = slice(n * 256, (n + 1) * 256)
            total = acc[rows_of(m), cols] + jnp.dot(ab[...], d0[:, cols], preferred_element_type=F32)
            dense[rows_of(m), cols] = total.astype(BF)
        for local, away in results(m):
            away.start()
            local.start()

    def loop4(jj, _):
        m = 2 * jj
        fill(asec, 2, m + 1, [(ab1, 0)])
        pass4(m, ab0)
        fill(asec, 2, jnp.minimum(m + 2, 7), [(ab0, 0)])
        pass4(m + 1, ab1)
        return 0

    lax.fori_loop(0, 4, loop4, 0)

    def finish(m, _):
        for local, away in results(m):
            local.wait()
            away.wait()
        return 0

    lax.fori_loop(0, 8, finish, 0)
    for copy in sent:
        copy.wait_send()


def per_device(local_tiles, local_cols, section_tiles, section_cols, owners, prol_tiles, prol_cols):
    slots = jnp.arange(RB, dtype=jnp.int32)
    k = local_cols.shape[1]
    place = (slots[:, None] * k + jnp.arange(k, dtype=jnp.int32)[None, :])[:, :, None]
    local = jnp.min(jnp.where(local_cols[:, :, None] == slots, place, RB * k), axis=1)
    ks = section_cols.shape[2]
    place = jnp.arange(RB * GROUPS * ks, dtype=jnp.int32).reshape(RB, GROUPS, ks)[:, :, :, None]
    section = jnp.min(jnp.where(section_cols[:, :, :, None] == slots, place, RB * k), axis=2)
    table = jnp.concatenate([local.reshape(-1), section.transpose(1, 0, 2).reshape(-1), owners])
    meta = jnp.where(jnp.arange(128)[None, :] < T, prol_cols[:, 0:1], prol_cols[:, 1:2]).astype(BF)

    vmem = pl.BlockSpec(memory_space=pltpu.VMEM)
    smem = pl.BlockSpec(memory_space=pltpu.SMEM)
    hbm = pl.BlockSpec(memory_space=pl.ANY)
    v = pltpu.VMEM
    copies = 64
    return pl.pallas_call(
        kernel,
        out_shape=jax.ShapeDtypeStruct((ROWS, 2048), BF),
        in_specs=[smem, vmem, hbm, hbm, hbm],
        out_specs=hbm,
        scratch_shapes=[
            v((64, T, T), BF), v((769, T, T), BF), v((769, T, T), BF),
            v((ROWS, 128), BF), v((ROWS, 128), BF), v((RB, 128), BF),
            v((4, 256, 128), BF), v((4, 256, 128), BF), v((4, RB, 128), BF),
            v((2, 2, 256, 128), BF), v((2, RB, 128), BF),
            v((2, 2, 4, T, 128), BF), v((4, 2, RB, 128), BF),
            v((2, 2, T, 128), BF), v((2, RB, 128), BF),
            v((2, 4, 2, T, 128), BF), v((4, 2, RB, 128), BF),
            v((2, 2, ROWS, 128), BF), v((2, 2, RB, 128), BF), v((RB, 128), F32),
            v((ROWS, WIDE), BF), v((ROWS, WIDE), BF), v((ROWS, ROWS), BF),
            v((MT, ROWS), BF), v((MT, ROWS), BF), v((ROWS, WIDE), F32),
            pltpu.SemaphoreType.DMA((3,)),
            pltpu.SemaphoreType.DMA((copies,)), pltpu.SemaphoreType.DMA((copies,)),
            pltpu.SemaphoreType.DMA((8, 2)), pltpu.SemaphoreType.DMA((8, 2)), pltpu.SemaphoreType.DMA((8, 2)),
        ],
        compiler_params=pltpu.CompilerParams(
            collective_id=0, has_side_effects=True, vmem_limit_bytes=60 * 2**20
        ),
        name="galerkin",
    )(table, meta, prol_tiles.reshape(64, T, T), local_tiles.reshape(768, T, T), section_tiles.reshape(768, T, T))


def solution(mesh):
    in_specs = (
        P("rows", None, None, None),
        P("rows", None),
        P("rows", None, None, None, None),
        P("rows", None, None),
        P(),
        P("rows", "cols", None, None),
        P("rows", "cols"),
    )
    return jax.shard_map(
        per_device, mesh=mesh, in_specs=in_specs, out_specs=P("rows", None), check_vma=False
    )
```

time: 440 us -> 90.4 us (0.21)
  waiting for transfers between devices: 253 us -> 0 us
  local copies, waits for them, and re-layouts: 98.9 us -> 10.8 us
  Pallas kernels: 0 us -> 76.6 us
  matrix products: 67.7 us -> 0 us
  between operations: 14.7 us -> 0.03 us
    psum x1 -> x0, waiting for transfers between devices: 169 us -> none  [broadcast(): return lax.psum(jnp.where(mine, array, jnp.zeros_like(array)), axis)]
    all_gather x1 -> x0, waiting for transfers between devices: 84.2 us -> none  [per_device(): result = lax.all_gather(result, 'cols', axis=1, tiled=True)]
    pallas_call x0 -> x1, Pallas kernels: none -> 76.6 us  [per_device(): pl.pallas_call(kernel, out_shape=jax.ShapeDtypeStruct((ROWS, 2048), BF),...]
    reshape x4 -> x2, local copies, waits for them, and re-layouts: 75.8 us -> 0.14 us  [the longest x1 0.07 us: per_device(): section.transpose(1, 0, 2).reshape(-1)]
    dot_general x7 -> x0, matrix products: 67.7 us -> none  [the longest x3 41.7 us: densify_stiff(): jnp.einsum('ikr,ikab->iarb', onehot, tiles, preferred_element_type=jnp.fl...]
    slice x3 -> x0, local copies, waits for them, and re-layouts: 13.5 us -> none  [the longest x1 12.9 us: per_device(): section_tiles[:, section]]
    unnamed x18 -> x3, local copies, waits for them, and re-layouts: 9.36 us -> 9.93 us
  transfers between devices with their start and end apart: 2 -> 0, of which waited for: 2 -> 0; matrix products, arithmetic and copies ran while one was open for 31% -> 0% of each run, Pallas kernels for 0% -> 0%
where the time goes in v1:
time: 90.4 us; the launch traced here: 90 us
  Pallas kernels  76.6 us (85%)
  local copies, waits for them, and re-layouts  10.8 us (12%)
  other arithmetic  2.59 us (3%)
    pallas_call x1, Pallas kernels, per_device(): pl.pallas_call(kernel, out_shape=jax.ShapeDtypeStruct((ROWS, 2048), BF),...  76.6 us
    unnamed x3, local copies, waits for them, and re-layouts  9.93 us

profile of v1, /device:TPU:1, one launch (start us, length us, event | category | flops | bytes accessed | tf_op | source)
XLA Modules:
  0.0 90.0 jit_solution(10659628261038759586)
XLA Ops:
  0.0 0.8 slice_bitcast_fusion.1
  0.8 0.7 select_convert_fusion.meta
  1.4 0.1 iota_add_fusion
  1.5 0.8 copy.12
  2.3 0.3 select_reduce_fusion.1
  2.6 0.1 reshape.64
  2.7 0.7 copy.13
  3.4 0.3 select_reduce_fusion
  3.7 0.1 reshape.65
  3.7 1.3 %pad_add_fusion.table = s32[3074]{0:T(1024)} fusion(s32[2]{0:T(128)} %param.11, s32[2048]{0:T(1024)S(1)} %reshape.65, s32[1024]{0:T(1024)S(1)} %reshape.64), kind=kLoop, calls=%fused_computation.4 | loop fusion | flops 6148 | bytes 24592 | tf_op jit(solution)/shard_map/concatenate | solution.py:326
  5.0 76.6 %galerkin.1 = bf16[2048,2048]{1,0:T(8,128)(2,1)} custom-call(s32[3074]{0:T(1024)} %pad_add_fusion.table, bf16[32,128]{1,0:T(8,128)(2,1)} %select_convert_fusion.meta, bf16[64,64,64]{2,1,0:T(8,128)(2,1)} %bitcast.10, bf16[768,64,64]{2,1,0:T(8,128)(2,1)} %bitcast.8, bf16[768,64,64]{2,1,0:T(8,128)(2,1)} %bitcast.9), custom_call_target="tpu_custom_call" | custom-call | tf_op jit(solution)/shard_map/galerkin/pallas_call | solution.py:334
  81.6 8.4 %copy.15 = bf16[2048,2048]{1,0:T(8,128)(2,1)} copy(bf16[2048,2048]{1,0:T(8,128)(2,1)} %galerkin.1) | data formatting | bytes 16777216
  (3 shorter events, 0.0 us)

commit v2 on v1

v2 whole, which is shorter than its diff:
```python
import jax
import jax.numpy as jnp
from jax import lax
from jax.experimental import pallas as pl
from jax.experimental.pallas import tpu as pltpu
from jax.sharding import PartitionSpec as P

MESH = pl.DeviceIdType.MESH
BF = jnp.bfloat16
F32 = jnp.float32
T = 64
RB = 32
MT = 256
ROWS = RB * T
HALF = 512
WIDE = 2 * HALF
GROUPS = 2
K = 24
KS = 12


def kernel(
    lcols, scols, pcols, owners, p_hbm, l_hbm, s_hbm, out,
    praw, aloc, asec, pc, pp, meta, mp, r1a, r1b, r1m, s1, s1m, r2_0, r2_1, r2m_0, r2m_1, s2, s2m,
    rx_0, rx_1, rxm_0, rxm_1, qc, qm, mf,
    d0, d1, ab0, ab1, acc, vtable, table,
    load_sem, send_sem, recv_sem, osend, orecv,
):
    r = lax.axis_index("rows")
    c = lax.axis_index("cols")
    y, xl, z = r // 8, (r // 4) % 2, r % 4
    xh, core = c // 2, c % 2
    x = xh * 2 + xl

    def y_peer(j):
        return (((y + j) % 4 * 2 + xl) * 4 + z, c)

    def z_peer(j):
        return ((y * 2 + xl) * 4 + (z + j) % 4, c)

    def x_peer(j):
        q = (x + j) % 4
        return ((y * 2 + q % 2) * 4 + z, (q // 2) * 2 + core)

    core_peer = (r, xh * 2 + 1 - core)
    r2, r2m, rx, rxm = (r2_0, r2_1), (r2m_0, r2m_1), (rx_0, rx_1), (rxm_0, rxm_1)

    load_p = pltpu.make_async_copy(p_hbm, praw, load_sem.at[0])
    load_l = pltpu.make_async_copy(l_hbm, aloc.at[:, pl.ds(0, K)], load_sem.at[1])
    load_s = [
        pltpu.make_async_copy(s_hbm.at[:, 0], asec.at[:, pl.ds(0, KS)], load_sem.at[2]),
        pltpu.make_async_copy(s_hbm.at[:, 1], aloc.at[:, pl.ds(0, KS)], load_sem.at[3]),
    ]
    load_p.start()
    load_l.start()
    load_s[0].start()

    barrier = pltpu.get_barrier_semaphore()
    for peer in [f(j) for f in (y_peer, z_peer, x_peer) for j in (1, 2, 3)] + [core_peer]:
        pl.semaphore_signal(barrier, inc=1, device_id=peer, device_id_type=MESH)

    sub = lax.broadcasted_iota(jnp.int32, (RB, RB), 0)
    lane = lax.broadcasted_iota(jnp.int32, (RB, RB), 1)
    first, second = [
        jnp.sum(jnp.where(sub == lane, pcols[j : j + 1, :], 0).astype(F32), axis=1, keepdims=True) for j in range(2)
    ]
    meta[...] = jnp.where(lax.broadcasted_iota(jnp.int32, (RB, 128), 1) < T, first, second).astype(BF)

    def owner(s):
        o = owners[s]
        return o // 8, (o // 4) % 2, o % 4

    sent = []

    def remote(src, dst, peer):
        i = len(sent)
        copy = pltpu.make_async_remote_copy(
            src_ref=src, dst_ref=dst, send_sem=send_sem.at[i], recv_sem=recv_sem.at[i],
            device_id=peer, device_id_type=MESH,
        )
        copy.start()
        sent.append(copy)
        return copy

    def rows_at(base, index, size):
        return pl.ds(pl.multiple_of(base + index * size, size), size)

    load_p.wait()

    def compact(k, _):
        rows = pl.ds(pl.multiple_of(k * T, T), T)
        pc[rows, :] = jnp.concatenate([praw[k, 0], praw[k, 1]], axis=1)
        return 0

    lax.fori_loop(0, RB, compact, 0, unroll=4)
    pl.semaphore_wait(barrier, 10)

    stage1 = []
    for j in (1, 2, 3):
        stage1.append(remote(pc.at[rows_at(0, (y + j) % 4, 256)], r1a.at[j], y_peer(j)))
        stage1.append(remote(pc.at[rows_at(1024, (z + j) % 4, 256)], r1b.at[j], z_peer(j)))
        stage1.append(remote(meta, r1m.at[j], y_peer(j)))
    half = pl.ds(0, 1024)
    partner = [remote(pc.at[half], pp.at[half], x_peer(2)), remote(meta, mp, x_peer(2))]
    r1a[0] = pc[rows_at(0, y, 256)]
    r1b[0] = pc[rows_at(1024, z, 256)]
    r1m[0] = meta[...]

    stage2, stage3, stage4, stage5 = [[], []], [[], []], [[], []], [[], []]

    def step1():
        for copy in stage1:
            copy.wait_recv()
        for s in range(GROUPS):
            oy, ox, oz = owner(s)
            s1[s, 0] = r1a[(y + 4 - oy) % 4]
            s1[s, 1] = r1b[(z + 4 - oz) % 4]
            s1m[s] = r1m[(y + 4 - oy) % 4]
            for j in (1, 2, 3):
                stage2[s].append(remote(s1.at[s, 0, rows_at(0, (z + j) % 4, T)], r2[s].at[0, j], z_peer(j)))
                stage2[s].append(remote(s1.at[s, 1, rows_at(0, (y + j) % 4, T)], r2[s].at[1, j], y_peer(j)))
                stage2[s].append(remote(s1m.at[s], r2m[s].at[j], z_peer(j)))
            r2[s][0, 0] = s1[s, 0, rows_at(0, z, T)]
            r2[s][1, 0] = s1[s, 1, rows_at(0, y, T)]
            r2m[s][0] = s1m[s]

    def step2(s):
        for copy in stage2[s]:
            copy.wait_recv()
        oy, ox, oz = owner(s)
        s2[s, 0] = r2[s][0, (z + 4 - oz) % 4]
        s2[s, 1] = r2[s][1, (y + 4 - oy) % 4]
        s2m[s] = r2m[s][(z + 4 - oz) % 4]
        for j in (1, 2, 3):
            stage3[s].append(remote(s2.at[s], rx[s].at[j], x_peer(j)))
            stage3[s].append(remote(s2m.at[s], rxm[s].at[j], x_peer(j)))
        rx[s][0] = s2[s]
        rxm[s][0] = s2m[s]

    def step3(s):
        for copy in stage3[s]:
            copy.wait_recv()
        oy, ox, oz = owner(s)
        for h in range(2):
            slot = (x + 4 - (h * 2 + ox)) % 4
            qc[s, h, rows_at(0, y * 4 + z, T)] = rx[s][slot, 0]
            qc[s, h, rows_at(1024, z * 4 + y, T)] = rx[s][slot, 1]
            qm[s, h] = rxm[s][slot]
        first = qc.at[s, :, rows_at(0, y * 4 + z, T)]
        second = qc.at[s, :, rows_at(1024, z * 4 + y, T)]
        for j in (1, 2, 3):
            stage4[s].append(remote(first, first, z_peer(j)))
            stage4[s].append(remote(second, second, y_peer(j)))

    def step4(s):
        for copy in stage4[s]:
            copy.wait_recv()
        first = qc.at[s, :, rows_at(0, y, 256)]
        second = qc.at[s, :, rows_at(1024, z, 256)]
        for j in (1, 2, 3):
            stage5[s].append(remote(first, first, y_peer(j)))
            stage5[s].append(remote(second, second, z_peer(j)))

    def step5(s):
        for copy in stage5[s]:
            copy.wait_recv()

    tile = jnp.full((RB, RB), K, jnp.int32)
    for k in range(K):
        tile = jnp.where(lcols[k : k + 1, :] == sub, k, tile)
    vtable[0:RB, 0:RB] = tile
    for s in range(GROUPS):
        tile = jnp.full((RB, RB), K if s else KS, jnp.int32)
        for k in range(KS):
            tile = jnp.where(scols[k][s : s + 1, :] == sub, k, tile)
        vtable[RB * (s + 1) : RB * (s + 2), 0:RB] = tile
    to_scalar = pltpu.make_async_copy(vtable, table, load_sem.at[4])
    to_scalar.start()

    def clear(i, _):
        aloc[i, K] = jnp.zeros((T, T), BF)
        asec[i, KS] = jnp.zeros((T, T), BF)
        return 0

    lax.fori_loop(0, RB, clear, 0, unroll=4)

    side = (lax.broadcasted_iota(jnp.int32, (16, 128), 1) >= T).astype(F32)
    slots = [(side + 2.0 * p).astype(BF) for p in range(4)]

    def spread(src, cols, dst, h):
        mf[...] = cols.astype(F32)

        def body(k, _):
            row = jnp.broadcast_to(mf[pl.ds(k, 1), :], (16, 128))
            swapped = jnp.concatenate([row[:, T:], row[:, :T]], axis=1).astype(BF)
            row = row.astype(BF)
            masks = [(row == slots[p], swapped == slots[p]) for p in range(4)]
            for q in range(4):
                rows = pl.ds(pl.multiple_of(k * T + q * 16, 16), 16)
                t = src(rows)
                u = jnp.concatenate([t[:, T:], t[:, :T]], axis=1)
                for p in range(4):
                    dst[rows, h * HALF + p * 128 : h * HALF + (p + 1) * 128] = jnp.where(
                        masks[p][0], t, jnp.where(masks[p][1], u, jnp.zeros_like(t))
                    )
            return 0

        lax.fori_loop(0, RB, body, 0, unroll=8)

    def fill(src, which, m, dst):
        for b in range(4):
            i = m * 4 + b
            for p in range(16):
                dst[b * T : (b + 1) * T, p * 128 : (p + 1) * 128] = jnp.concatenate(
                    [src[i, table[which * RB + 2 * p, i]], src[i, table[which * RB + 2 * p + 1, i]]], axis=1
                )

    def rows_of(m):
        return pl.ds(pl.multiple_of(m * MT, MT), MT)

    def multiply(src, which, use, points=()):
        fill(src, which, 0, ab0)

        def pair(jj, _):
            m = 2 * jj
            fill(src, which, m + 1, ab1)
            use(m, ab0)
            fill(src, which, jnp.minimum(m + 2, 7), ab0)
            use(m + 1, ab1)
            return 0

        start = 0
        for stop, point in points:
            lax.fori_loop(start, stop, pair, 0)
            point()
            start = stop
        lax.fori_loop(start, 4, pair, 0)

    spread(lambda rows: pc[rows, :], meta[...], d0, 0)
    to_scalar.wait()
    load_l.wait()

    def pass1(m, ab):
        for n in range(2):
            cols = slice(n * 256, (n + 1) * 256)
            acc[rows_of(m), cols] = jnp.dot(ab[...], d0[:, cols], preferred_element_type=F32)

    other = pl.ds(1024, 1024)

    def point2():
        step2(0)
        partner.append(remote(pc.at[other], pp.at[other], x_peer(2)))

    def point3():
        step2(1)
        step3(0)

    multiply(aloc, 0, pass1, [(1, step1), (2, point2), (3, point3)])
    step4(0)
    step3(1)

    for copy in partner:
        copy.wait_recv()
    spread(lambda rows: pp[rows, :], mp[...], d0, 1)

    def pass2(m, ab):
        for n in range(2, 4):
            cols = slice(n * 256, (n + 1) * 256)
            acc[rows_of(m), cols] = jnp.dot(ab[...], d0[:, cols], preferred_element_type=F32)

    multiply(aloc, 0, pass2)

    load_s[1].start()
    load_s[0].wait()
    sides = [xh, 1 - xh]
    step5(0)
    step4(1)
    for h in range(2):
        spread(lambda rows: qc[0, sides[h], rows, :], qm[0, sides[h]], d1, h)

    def pass3(m, ab):
        for n in range(4):
            cols = slice(n * 256, (n + 1) * 256)
            acc[rows_of(m), cols] += jnp.dot(ab[...], d1[:, cols], preferred_element_type=F32)

    multiply(asec, 1, pass3)

    load_s[1].wait()
    step5(1)
    for h in range(2):
        spread(lambda rows: qc[1, sides[h], rows, :], qm[1, sides[h]], d0, h)

    def place(m, h):
        return rows_of(m), pl.ds(pl.multiple_of((sides[h] * 2 + core) * HALF, HALF), HALF)

    def result(m, h):
        ref = out.at[place(m, h)]
        return pltpu.make_async_remote_copy(
            src_ref=ref, dst_ref=ref, send_sem=osend.at[m, h], recv_sem=orecv.at[m, h],
            device_id=core_peer, device_id_type=MESH,
        )

    def pass4(m, ab):
        for h in range(2):
            cols = slice(h * HALF, (h + 1) * HALF)
            total = acc[rows_of(m), cols] + jnp.dot(ab[...], d0[:, cols], preferred_element_type=F32)
            out[place(m, h)] = total.astype(BF)
            result(m, h).start()

    multiply(aloc, 2, pass4)

    def finish(m, _):
        for h in range(2):
            result(m, h).wait()
        return 0

    lax.fori_loop(0, 8, finish, 0)
    for copy in sent:
        copy.wait_send()


def per_device(local_tiles, local_cols, section_tiles, section_cols, owners, prol_tiles, prol_cols):
    vmem = pl.BlockSpec(memory_space=pltpu.VMEM)
    smem = pl.BlockSpec(memory_space=pltpu.SMEM)
    hbm = pl.BlockSpec(memory_space=pl.ANY)
    v = pltpu.VMEM
    copies = 72
    return pl.pallas_call(
        kernel,
        out_shape=pltpu.VMEM((ROWS, 2048), BF),
        in_specs=[vmem, vmem, vmem, smem, hbm, hbm, hbm],
        out_specs=pl.BlockSpec(memory_space=pltpu.VMEM),
        scratch_shapes=[
            v((RB, 2, T, T), BF), v((RB, K + 1, T, T), BF), v((RB, KS + 1, T, T), BF),
            v((ROWS, 128), BF), v((ROWS, 128), BF), v((RB, 128), BF), v((RB, 128), BF),
            v((4, 256, 128), BF), v((4, 256, 128), BF), v((4, RB, 128), BF),
            v((2, 2, 256, 128), BF), v((2, RB, 128), BF),
            v((2, 4, T, 128), BF), v((2, 4, T, 128), BF), v((4, RB, 128), BF), v((4, RB, 128), BF),
            v((2, 2, T, 128), BF), v((2, RB, 128), BF),
            v((4, 2, T, 128), BF), v((4, 2, T, 128), BF), v((4, RB, 128), BF), v((4, RB, 128), BF),
            v((2, 2, ROWS, 128), BF), v((2, 2, RB, 128), BF), v((RB, 128), F32),
            v((ROWS, WIDE), BF), v((ROWS, WIDE), BF),
            v((MT, ROWS), BF), v((MT, ROWS), BF), v((ROWS, WIDE), F32),
            v((3 * RB, 128), jnp.int32), pltpu.SMEM((3 * RB, 128), jnp.int32),
            pltpu.SemaphoreType.DMA((5,)),
            pltpu.SemaphoreType.DMA((copies,)), pltpu.SemaphoreType.DMA((copies,)),
            pltpu.SemaphoreType.DMA((8, 2)), pltpu.SemaphoreType.DMA((8, 2)),
        ],
        compiler_params=pltpu.CompilerParams(
            collective_id=0, has_side_effects=True, vmem_limit_bytes=46 * 2**20
        ),
        name="galerkin",
    )(local_cols.T, section_cols.transpose(2, 1, 0), prol_cols.T, owners, prol_tiles, local_tiles, section_tiles)


def solution(mesh):
    in_specs = (
        P("rows", None, None, None),
        P("rows", None),
        P("rows", None, None, None, None),
        P("rows", None, None),
        P(),
        P("rows", "cols", None, None),
        P("rows", "cols"),
    )
    return jax.shard_map(
        per_device, mesh=mesh, in_specs=in_specs, out_specs=P("rows", None), check_vma=False
    )
```

time: 90.4 us -> 72.2 us (0.80)
  Pallas kernels: 76.6 us -> 68.6 us
  local copies, waits for them, and re-layouts: 10.8 us -> 3.4 us
  other arithmetic: 2.59 us -> 0 us
    pallas_call x1, Pallas kernels: 76.6 us -> 68.6 us  [per_device(): pl.pallas_call(kernel, out_shape=pltpu.VMEM((ROWS, 2048), BF), in_specs=[...]
    unnamed x3 -> x1, local copies, waits for them, and re-layouts: 9.93 us -> 3.4 us
    concatenate x1 -> x0, other arithmetic: 1.27 us -> none  [per_device(): jnp.concatenate([local.reshape(-1), section.transpose(1, 0, 2).reshape(-1...]
where the time goes in v2:
time: 72.2 us; the launch traced here: 72 us
  Pallas kernels  68.6 us (95%)
  local copies, waits for them, and re-layouts  3.4 us (5%)
    pallas_call x1, Pallas kernels, per_device(): pl.pallas_call(kernel, out_shape=pltpu.VMEM((ROWS, 2048), BF), in_specs=[...  68.6 us
    unnamed x1, local copies, waits for them, and re-layouts  3.4 us

profile of v2, /device:TPU:1, one launch (start us, length us, event | category | flops | bytes accessed | tf_op | source)
XLA Modules:
  0.0 72.0 jit_solution(7106323818627125255)
XLA Ops:
  0.0 68.6 %galerkin.1 = bf16[2048,2048]{1,0:T(8,128)(2,1)S(1)} custom-call(s32[24,32]{1,0:T(8,128)} %bitcast.3, s32[12,2,32]{2,1,0:T(2,128)} %bitcast.4, s32[2,32]{1,0:T(2,128)} %bitcast.5, s32[2]{0:T(128)} %owners.1, bf16[32,2,64,64]{3,2,1,0:T(8,128)(2,1)} %p_hbm.1, bf16[32,24,64,64]{3,2,1,0:T(8,128)(2,1)} %l_hbm.1, bf16[32,2,12,64,64]{4,3,2,1,0:T(8,128)(2,1)} %s_hbm.1), custom_call_target="tpu_custom_call" | custom-call | tf_op jit(solution)/shard_map/galerkin/pallas_call | solution.py:328
  68.6 3.4 %copy.9 = bf16[2048,2048]{1,0:T(8,128)(2,1)} copy(bf16[2048,2048]{1,0:T(8,128)(2,1)S(1)} %galerkin.1) | data formatting | bytes 16777216

commit v3 on v2

v3 whole, which is shorter than its diff:
```python
import jax
import jax.numpy as jnp
from jax import lax
from jax.experimental import pallas as pl
from jax.experimental.pallas import tpu as pltpu
from jax.sharding import PartitionSpec as P

MESH = pl.DeviceIdType.MESH
BF = jnp.bfloat16
F32 = jnp.float32
T = 64
RB = 32
K = 24
KS = 12
MT = 256
ROWS = RB * T
DEPTH = ROWS // 2
HALF = 512
WIDE = 2 * HALF
UNITS = [(0, 0), (0, 1), (1, 0), (1, 1)]
COPIES = 128


def kernel(lcols, scols, pcols, owners, p_hbm, l_hbm, s_hbm, out, *scratch):
    refs = iter(scratch)

    def take(n):
        return [next(refs) for _ in range(n)]

    praw, aloc, asec, pc, pp, meta, mp, mown, mpart, mq = take(10)
    r1a, r1b = take(2), take(2)
    r1m, s1, s1m = take(3)
    r2, r2m = take(4), take(2)
    s2, s2m = take(2)
    rx, rxm = take(4), take(2)
    qc, d0, d1, ab0, ab1, acc, vtable, table = take(8)
    load_sem, send_sem, recv_sem, osend, orecv = take(5)

    r = lax.axis_index("rows")
    c = lax.axis_index("cols")
    y, xl, z = r // 8, (r // 4) % 2, r % 4
    xh, core = c // 2, c % 2
    x = xh * 2 + xl
    sides = [xh, 1 - xh]

    def y_peer(j):
        return (((y + j) % 4 * 2 + xl) * 4 + z, c)

    def z_peer(j):
        return ((y * 2 + xl) * 4 + (z + j) % 4, c)

    def x_peer(j):
        q = (x + j) % 4
        return ((y * 2 + q % 2) * 4 + z, (q // 2) * 2 + core)

    core_peer = (r, xh * 2 + 1 - core)

    load_p = pltpu.make_async_copy(p_hbm, praw, load_sem.at[0])
    load_l = pltpu.make_async_copy(l_hbm, aloc.at[:, pl.ds(0, K)], load_sem.at[1])
    load_s = [
        pltpu.make_async_copy(s_hbm.at[:, 0], asec.at[:, pl.ds(0, KS)], load_sem.at[2]),
        pltpu.make_async_copy(s_hbm.at[:, 1], aloc.at[:, pl.ds(0, KS)], load_sem.at[3]),
    ]
    load_p.start()
    load_l.start()
    load_s[0].start()

    barrier = pltpu.get_barrier_semaphore()
    for peer in [f(j) for f in (y_peer, z_peer, x_peer) for j in (1, 2, 3)] + [core_peer]:
        pl.semaphore_signal(barrier, inc=1, device_id=peer, device_id_type=MESH)

    sub = lax.broadcasted_iota(jnp.int32, (RB, RB), 0)
    lane = lax.broadcasted_iota(jnp.int32, (RB, RB), 1)
    first, second = [
        jnp.sum(jnp.where(sub == lane, pcols[j : j + 1, :], 0).astype(F32), axis=1, keepdims=True) for j in range(2)
    ]
    mown[...] = jnp.where(lax.broadcasted_iota(jnp.int32, (RB, 128), 1) < T, first, second)
    meta[...] = mown[...].astype(BF)

    def owner(s):
        o = owners[s]
        return o // 8, (o // 4) % 2, o % 4

    sent = []

    def remote(src, dst, peer):
        i = len(sent)
        copy = pltpu.make_async_remote_copy(
            src_ref=src, dst_ref=dst, send_sem=send_sem.at[i], recv_sem=recv_sem.at[i],
            device_id=peer, device_id_type=MESH,
        )
        copy.start()
        sent.append(copy)
        return copy

    def rows_at(base, index, size):
        return pl.ds(pl.multiple_of(base + index * size, size), size)

    load_p.wait()

    def compact(k, _):
        rows = pl.ds(pl.multiple_of(k * T, T), T)
        pc[rows, :] = jnp.concatenate([praw[k, 0], praw[k, 1]], axis=1)
        return 0

    lax.fori_loop(0, RB, compact, 0, unroll=4)
    pl.semaphore_wait(barrier, 10)

    base_a = [u * DEPTH for u in range(2)]
    base_b = [u * DEPTH + DEPTH // 2 for u in range(2)]
    stage1 = [[], []]
    for h in range(2):
        for j in (1, 2, 3):
            stage1[h].append(remote(pc.at[rows_at(base_a[h], (y + j) % 4, 128)], r1a[h].at[j], y_peer(j)))
            stage1[h].append(remote(pc.at[rows_at(base_b[h], (z + j) % 4, 128)], r1b[h].at[j], z_peer(j)))
            if h == 0:
                stage1[h].append(remote(meta, r1m.at[j], y_peer(j)))
    halves = [pl.ds(0, DEPTH), pl.ds(DEPTH, DEPTH)]
    partner = [[remote(meta, mp, x_peer(2)), remote(pc.at[halves[0]], pp.at[halves[0]], x_peer(2))]]
    for h in range(2):
        r1a[h][0] = pc[rows_at(base_a[h], y, 128)]
        r1b[h][0] = pc[rows_at(base_b[h], z, 128)]
    r1m[0] = meta[...]

    stage2, stage3, stage4, stage5 = [[[] for _ in UNITS] for _ in range(4)]

    def step1(h):
        for copy in stage1[h]:
            copy.wait_recv()
        for s in range(2):
            u = 2 * s + h
            oy, ox, oz = owner(s)
            s1[u, 0] = r1a[h][(y + 4 - oy) % 4]
            s1[u, 1] = r1b[h][(z + 4 - oz) % 4]
            if h == 0:
                s1m[s] = r1m[(y + 4 - oy) % 4]
            for j in (1, 2, 3):
                stage2[u].append(remote(s1.at[u, 0, rows_at(0, (z + j) % 4, 32)], r2[u].at[0, j], z_peer(j)))
                stage2[u].append(remote(s1.at[u, 1, rows_at(0, (y + j) % 4, 32)], r2[u].at[1, j], y_peer(j)))
                if h == 0:
                    stage2[u].append(remote(s1m.at[s], r2m[s].at[j], z_peer(j)))
            r2[u][0, 0] = s1[u, 0, rows_at(0, z, 32)]
            r2[u][1, 0] = s1[u, 1, rows_at(0, y, 32)]
            if h == 0:
                r2m[s][0] = s1m[s]

    def step2(u):
        s, h = UNITS[u]
        for copy in stage2[u]:
            copy.wait_recv()
        oy, ox, oz = owner(s)
        s2[u, 0] = r2[u][0, (z + 4 - oz) % 4]
        s2[u, 1] = r2[u][1, (y + 4 - oy) % 4]
        for j in (1, 2, 3):
            stage3[u].append(remote(s2.at[u], rx[u].at[j], x_peer(j)))
        rx[u][0] = s2[u]
        if h == 0:
            s2m[s] = r2m[s][(z + 4 - oz) % 4]
            for j in (1, 2, 3):
                stage3[u].append(remote(s2m.at[s], rxm[s].at[j], x_peer(j)))
            rxm[s][0] = s2m[s]

    def step3(u):
        s, h = UNITS[u]
        for copy in stage3[u]:
            copy.wait_recv()
        oy, ox, oz = owner(s)
        mine_a = rows_at(base_a[h], y * 4 + z, 32)
        mine_b = rows_at(base_b[h], z * 4 + y, 32)
        for side in range(2):
            slot = (x + 4 - (side * 2 + ox)) % 4
            qc[s, side, mine_a] = rx[u][slot, 0]
            qc[s, side, mine_b] = rx[u][slot, 1]
            if h == 0:
                mq[s, side] = rxm[s][slot].astype(F32)
        piece_a, piece_b = qc.at[s, :, mine_a], qc.at[s, :, mine_b]
        for j in (1, 2, 3):
            stage4[u].append(remote(piece_a, piece_a, z_peer(j)))
            stage4[u].append(remote(piece_b, piece_b, y_peer(j)))

    def step4(u):
        s, h = UNITS[u]
        for copy in stage4[u]:
            copy.wait_recv()
        piece_a = qc.at[s, :, rows_at(base_a[h], y, 128)]
        piece_b = qc.at[s, :, rows_at(base_b[h], z, 128)]
        for j in (1, 2, 3):
            stage5[u].append(remote(piece_a, piece_a, y_peer(j)))
            stage5[u].append(remote(piece_b, piece_b, z_peer(j)))

    def step5(u):
        for copy in stage5[u]:
            copy.wait_recv()

    tile = jnp.full((RB, RB), K, jnp.int32)
    for k in range(K):
        tile = jnp.where(lcols[k : k + 1, :] == sub, k, tile)
    vtable[0:RB, 0:RB] = tile
    for s in range(2):
        tile = jnp.full((RB, RB), K if s else KS, jnp.int32)
        for k in range(KS):
            tile = jnp.where(scols[k][s : s + 1, :] == sub, k, tile)
        vtable[RB * (s + 1) : RB * (s + 2), 0:RB] = tile
    to_scalar = pltpu.make_async_copy(vtable, table, load_sem.at[4])
    to_scalar.start()

    def clear(i, _):
        aloc[i, K] = jnp.zeros((T, T), BF)
        asec[i, KS] = jnp.zeros((T, T), BF)
        return 0

    lax.fori_loop(0, RB, clear, 0, unroll=4)

    side_of = (lax.broadcasted_iota(jnp.int32, (16, 128), 1) >= T).astype(F32)
    slots = [(side_of + 2.0 * p).astype(BF) for p in range(4)]

    def spread_row(k, src, cols, dst, h):
        row = jnp.broadcast_to(cols(k), (16, 128))
        swapped = jnp.concatenate([row[:, T:], row[:, :T]], axis=1).astype(BF)
        row = row.astype(BF)
        masks = [(row == slots[p], swapped == slots[p]) for p in range(4)]
        for q in range(4):
            rows = pl.ds(pl.multiple_of(k * T + q * 16, 16), 16)
            t = src(rows)
            u = jnp.concatenate([t[:, T:], t[:, :T]], axis=1)
            for p in range(4):
                dst[rows, h * HALF + p * 128 : h * HALF + (p + 1) * 128] = jnp.where(
                    masks[p][0], t, jnp.where(masks[p][1], u, jnp.zeros_like(t))
                )

    def spread(start, stop, src, cols, dst, h):
        def body(k, _):
            spread_row(k, src, cols, dst, h)
            return 0

        lax.fori_loop(start, stop, body, 0, unroll=8)

    def fill(src, which, m, dst, pairs):
        for b in range(4):
            i = m * 4 + b
            for n, p in enumerate(pairs):
                dst[b * T : (b + 1) * T, n * 128 : (n + 1) * 128] = jnp.concatenate(
                    [src[i, table[which * RB + 2 * p, i]], src[i, table[which * RB + 2 * p + 1, i]]], axis=1
                )

    def rows_of(m):
        return pl.ds(pl.multiple_of(m * MT, MT), MT)

    def multiply(src, which, pairs, use, points=(), beside=None):
        fill(src, which, 0, ab0, pairs)

        def run(start, stop, extra):
            def body(jj, _):
                m = 2 * jj
                fill(src, which, m + 1, ab1, pairs)
                use(m, ab0)
                if extra is not None:
                    extra(jj - 2)
                fill(src, which, jnp.minimum(m + 2, 7), ab0, pairs)
                use(m + 1, ab1)
                return 0

            if stop > start:
                lax.fori_loop(start, stop, body, 0)

        at = 0
        for stop, point in points:
            run(at, stop, beside if at >= 2 else None)
            point()
            at = stop
        run(at, 4, beside if at >= 2 else None)

    def block(ab, depth, cols, dst, top):
        return jnp.dot(ab[:, :depth], dst[top : top + depth, cols], preferred_element_type=F32)

    def steps(*calls):
        def point():
            for step, arg in calls:
                step(arg)

        return point

    spread(0, RB, lambda rows: pc[rows, :], lambda k: mown[pl.ds(k, 1), :], d0, 0)
    to_scalar.wait()
    load_l.wait()

    def pass1(m, ab):
        for n in range(2):
            cols = slice(n * 256, (n + 1) * 256)
            acc[rows_of(m), cols] = block(ab, ROWS, cols, d0, 0)

    def rest(_):
        partner.append([remote(pc.at[halves[1]], pp.at[halves[1]], x_peer(2))])

    multiply(
        aloc, 0, range(16), pass1,
        [(1, steps((step1, 0))), (2, steps((step1, 1))), (3, steps((step2, 0), (rest, 0)))],
    )
    step2(1)

    def pass2(h):
        def use(m, ab):
            for n in range(2, 4):
                cols = slice(n * 256, (n + 1) * 256)
                part = block(ab, DEPTH, cols, d0, h * DEPTH)
                if h:
                    part += acc[rows_of(m), cols]
                acc[rows_of(m), cols] = part

        return use

    def begin(h):
        for copy in partner[h]:
            copy.wait_recv()
        if h == 0:
            mpart[...] = mp[...].astype(F32)
        spread(h * 16, h * 16 + 16, lambda rows: pp[rows, :], lambda k: mpart[pl.ds(k, 1), :], d0, 1)

    begin(0)
    multiply(aloc, 0, range(8), pass2(0), [(1, steps((step3, 0))), (3, steps((step3, 1), (step2, 2)))])
    step4(0)
    step2(3)
    begin(1)
    multiply(
        aloc, 0, range(8, 16), pass2(1), [(1, steps((step4, 1), (step3, 2))), (3, steps((step3, 3), (step4, 2)))]
    )
    load_s[1].start()
    load_s[0].wait()

    dense = [d1, d1, d0, d0]

    def spread_unit(u, k, h):
        s, half = UNITS[u]
        spread_row(
            half * 16 + k, lambda rows: qc[s, sides[h], rows, :], lambda k: mq[s, sides[h], pl.ds(k, 1), :], dense[u], h
        )

    def ahead(u):
        def extra(part):
            for k in range(8):
                for h in range(2):
                    spread_unit(u, part * 8 + k, h)

        return extra

    def place(m, h):
        return rows_of(m), pl.ds(pl.multiple_of((sides[h] * 2 + core) * HALF, HALF), HALF)

    def result(m, h):
        ref = out.at[place(m, h)]
        return pltpu.make_async_remote_copy(
            src_ref=ref, dst_ref=ref, send_sem=osend.at[m, h], recv_sem=orecv.at[m, h],
            device_id=core_peer, device_id_type=MESH,
        )

    def pass3(u):
        top = UNITS[u][1] * DEPTH

        def use(m, ab):
            for n in range(4):
                cols = slice(n * 256, (n + 1) * 256)
                acc[rows_of(m), cols] += block(ab, DEPTH, cols, dense[u], top)

        def last(m, ab):
            for h in range(2):
                cols = slice(h * HALF, (h + 1) * HALF)
                total = acc[rows_of(m), cols] + block(ab, DEPTH, cols, dense[u], top)
                out[place(m, h)] = total.astype(BF)
                result(m, h).start()

        return last if u == 3 else use

    step5(0)
    step4(3)
    for h in range(2):
        s, half = UNITS[0]
        spread(
            0, 16, lambda rows: qc[0, sides[h], rows, :], lambda k: mq[0, sides[h], pl.ds(k, 1), :], d1, h
        )
    for u, (s, half) in enumerate(UNITS):
        if u == 2:
            load_s[1].wait()
        more = u < 3
        multiply(
            aloc if s else asec, s + 1, range(half * 8, half * 8 + 8), pass3(u),
            [(2, steps((step5, u + 1)))] if more else (), ahead(u + 1) if more else None,
        )

    def finish(m, _):
        for h in range(2):
            result(m, h).wait()
        return 0

    lax.fori_loop(0, 8, finish, 0)
    for copy in sent:
        copy.wait_send()


def per_device(local_tiles, local_cols, section_tiles, section_cols, owners, prol_tiles, prol_cols):
    vmem = pl.BlockSpec(memory_space=pltpu.VMEM)
    smem = pl.BlockSpec(memory_space=pltpu.SMEM)
    hbm = pl.BlockSpec(memory_space=pl.ANY)

    def b(*shape):
        return pltpu.VMEM(shape, BF)

    def f(*shape):
        return pltpu.VMEM(shape, F32)

    return pl.pallas_call(
        kernel,
        out_shape=pltpu.VMEM((ROWS, 2048), BF),
        in_specs=[vmem, vmem, vmem, smem, hbm, hbm, hbm],
        out_specs=vmem,
        scratch_shapes=[
            b(RB, 2, T, T), b(RB, K + 1, T, T), b(RB, KS + 1, T, T), b(ROWS, 128), b(ROWS, 128),
            b(RB, 128), b(RB, 128), f(RB, 128), f(RB, 128), f(2, 2, RB, 128),
            b(4, 128, 128), b(4, 128, 128), b(4, 128, 128), b(4, 128, 128),
            b(4, RB, 128), b(4, 2, 128, 128), b(2, RB, 128),
            *[b(2, 4, 32, 128) for _ in UNITS], b(4, RB, 128), b(4, RB, 128),
            b(4, 2, 32, 128), b(2, RB, 128),
            *[b(4, 2, 32, 128) for _ in UNITS], b(4, RB, 128), b(4, RB, 128),
            b(2, 2, ROWS, 128), b(ROWS, WIDE), b(ROWS, WIDE), b(MT, ROWS), b(MT, ROWS), f(ROWS, WIDE),
            pltpu.VMEM((3 * RB, 128), jnp.int32), pltpu.SMEM((3 * RB, 128), jnp.int32),
            pltpu.SemaphoreType.DMA((5,)),
            pltpu.SemaphoreType.DMA((COPIES,)), pltpu.SemaphoreType.DMA((COPIES,)),
            pltpu.SemaphoreType.DMA((8, 2)), pltpu.SemaphoreType.DMA((8, 2)),
        ],
        compiler_params=pltpu.CompilerParams(
            collective_id=0, has_side_effects=True, vmem_limit_bytes=46 * 2**20
        ),
        name="galerkin",
    )(local_cols.T, section_cols.transpose(2, 1, 0), prol_cols.T, owners, prol_tiles, local_tiles, section_tiles)


def solution(mesh):
    in_specs = (
        P("rows", None, None, None),
        P("rows", None),
        P("rows", None, None, None, None),
        P("rows", None, None),
        P(),
        P("rows", "cols", None, None),
        P("rows", "cols"),
    )
    return jax.shard_map(
        per_device, mesh=mesh, in_specs=in_specs, out_specs=P("rows", None), check_vma=False
    )
```

time: 72.2 us -> 68.7 us (0.952)
  Pallas kernels: 68.6 us -> 65.2 us
    pallas_call x1, Pallas kernels: 68.6 us -> 65.2 us  [per_device(): pl.pallas_call(kernel, out_shape=pltpu.VMEM((ROWS, 2048), BF), in_specs=[...]
where the time goes in v3:
time: 68.7 us; the launch traced here: 68.6 us
  Pallas kernels  65.2 us (95%)
  local copies, waits for them, and re-layouts  3.4 us (5%)
    pallas_call x1, Pallas kernels, per_device(): pl.pallas_call(kernel, out_shape=pltpu.VMEM((ROWS, 2048), BF), in_specs=[...  65.2 us
    unnamed x1, local copies, waits for them, and re-layouts  3.4 us

profile of v3, /device:TPU:1, one launch (start us, length us, event | category | flops | bytes accessed | tf_op | source)
XLA Modules:
  0.0 68.6 jit_solution(7925606474948583543)
XLA Ops:
  0.0 65.2 %galerkin.1 = bf16[2048,2048]{1,0:T(8,128)(2,1)S(1)} custom-call(s32[24,32]{1,0:T(8,128)} %bitcast.3, s32[12,2,32]{2,1,0:T(2,128)} %bitcast.4, s32[2,32]{1,0:T(2,128)} %bitcast.5, s32[2]{0:T(128)} %owners.1, bf16[32,2,64,64]{3,2,1,0:T(8,128)(2,1)} %p_hbm.1, bf16[32,24,64,64]{3,2,1,0:T(8,128)(2,1)} %l_hbm.1, bf16[32,2,12,64,64]{4,3,2,1,0:T(8,128)(2,1)} %s_hbm.1), custom_call_target="tpu_custom_call" | custom-call | tf_op jit(solution)/shard_map/galerkin/pallas_call | solution.py:410
  65.2 3.4 %copy.9 = bf16[2048,2048]{1,0:T(8,128)(2,1)} copy(bf16[2048,2048]{1,0:T(8,128)(2,1)S(1)} %galerkin.1) | data formatting | bytes 16777216

commit v4 on v3

--- a/solution.py
+++ b/solution.py
@@ -56,14 +56,19 @@
     core_peer = (r, xh * 2 + 1 - core)
 
     load_p = pltpu.make_async_copy(p_hbm, praw, load_sem.at[0])
-    load_l = pltpu.make_async_copy(l_hbm, aloc.at[:, pl.ds(0, K)], load_sem.at[1])
+    load_l = [
+        pltpu.make_async_copy(
+            l_hbm.at[pl.ds(8 * i, 8)], aloc.at[pl.ds(8 * i, 8), pl.ds(0, K)], load_sem.at[4 + i]
+        )
+        for i in range(4)
+    ]
     load_s = [
         pltpu.make_async_copy(s_hbm.at[:, 0], asec.at[:, pl.ds(0, KS)], load_sem.at[2]),
         pltpu.make_async_copy(s_hbm.at[:, 1], aloc.at[:, pl.ds(0, KS)], load_sem.at[3]),
     ]
     load_p.start()
-    load_l.start()
-    load_s[0].start()
+    for load in load_l:
+        load.start()
 
     barrier = pltpu.get_barrier_semaphore()
     for peer in [f(j) for f in (y_peer, z_peer, x_peer) for j in (1, 2, 3)] + [core_peer]:
@@ -201,7 +206,7 @@
         for k in range(KS):
             tile = jnp.where(scols[k][s : s + 1, :] == sub, k, tile)
         vtable[RB * (s + 1) : RB * (s + 2), 0:RB] = tile
-    to_scalar = pltpu.make_async_copy(vtable, table, load_sem.at[4])
+    to_scalar = pltpu.make_async_copy(vtable, table, load_sem.at[1])
     to_scalar.start()
 
     def clear(i, _):
@@ -282,7 +287,9 @@
 
     spread(0, RB, lambda rows: pc[rows, :], lambda k: mown[pl.ds(k, 1), :], d0, 0)
     to_scalar.wait()
-    load_l.wait()
+    for load in load_l:
+        load.wait()
+    load_s[0].start()
 
     def pass1(m, ab):
         for n in range(2):
@@ -294,7 +301,7 @@
 
     multiply(
         aloc, 0, range(16), pass1,
-        [(1, steps((step1, 0))), (2, steps((step1, 1))), (3, steps((step2, 0), (rest, 0)))],
+        [(1, steps((step1, 0), (rest, 0))), (2, steps((step1, 1))), (3, steps((step2, 0)))],
     )
     step2(1)
 
@@ -322,8 +329,9 @@
     step2(3)
     begin(1)
     multiply(
-        aloc, 0, range(8, 16), pass2(1), [(1, steps((step4, 1), (step3, 2))), (3, steps((step3, 3), (step4, 2)))]
+        aloc, 0, range(8, 16), pass2(1), [(1, steps((step4, 1))), (3, steps((step3, 2)))]
     )
+    step3(3)
     load_s[1].start()
     load_s[0].wait()
 
@@ -354,37 +362,37 @@
         )
 
     def pass3(u):
-        top = UNITS[u][1] * DEPTH
-
         def use(m, ab):
             for n in range(4):
                 cols = slice(n * 256, (n + 1) * 256)
-                acc[rows_of(m), cols] += block(ab, DEPTH, cols, dense[u], top)
-
-        def last(m, ab):
-            for h in range(2):
-                cols = slice(h * HALF, (h + 1) * HALF)
-                total = acc[rows_of(m), cols] + block(ab, DEPTH, cols, dense[u], top)
-                out[place(m, h)] = total.astype(BF)
-                result(m, h).start()
-
-        return last if u == 3 else use
+                acc[rows_of(m), cols] += block(ab, DEPTH, cols, d1, u * DEPTH)
+
+        return use
+
+    def last(m, ab):
+        for h in range(2):
+            cols = slice(h * HALF, (h + 1) * HALF)
+            total = acc[rows_of(m), cols] + block(ab, ROWS, cols, d0, 0)
+            out[place(m, h)] = total.astype(BF)
+            result(m, h).start()
+
+    def spread_all(u):
+        s, half = UNITS[u]
+        for h in range(2):
+            spread(
+                half * 16, half * 16 + 16, lambda rows: qc[s, sides[h], rows, :],
+                lambda k: mq[s, sides[h], pl.ds(k, 1), :], dense[u], h,
+            )
 
     step5(0)
+    spread_all(0)
+    multiply(asec, 1, range(8), pass3(0), [(2, steps((step5, 1), (step4, 2)))], ahead(1))
     step4(3)
-    for h in range(2):
-        s, half = UNITS[0]
-        spread(
-            0, 16, lambda rows: qc[0, sides[h], rows, :], lambda k: mq[0, sides[h], pl.ds(k, 1), :], d1, h
-        )
-    for u, (s, half) in enumerate(UNITS):
-        if u == 2:
-            load_s[1].wait()
-        more = u < 3
-        multiply(
-            aloc if s else asec, s + 1, range(half * 8, half * 8 + 8), pass3(u),
-            [(2, steps((step5, u + 1)))] if more else (), ahead(u + 1) if more else None,
-        )
+    multiply(asec, 1, range(8, 16), pass3(1), [(2, steps((step5, 2)))], ahead(2))
+    load_s[1].wait()
+    step5(3)
+    spread_all(3)
+    multiply(aloc, 2, range(16), last)
 
     def finish(m, _):
         for h in range(2):
@@ -422,7 +430,7 @@
             *[b(4, 2, 32, 128) for _ in UNITS], b(4, RB, 128), b(4, RB, 128),
             b(2, 2, ROWS, 128), b(ROWS, WIDE), b(ROWS, WIDE), b(MT, ROWS), b(MT, ROWS), f(ROWS, WIDE),
             pltpu.VMEM((3 * RB, 128), jnp.int32), pltpu.SMEM((3 * RB, 128), jnp.int32),
-            pltpu.SemaphoreType.DMA((5,)),
+            pltpu.SemaphoreType.DMA((8,)),
             pltpu.SemaphoreType.DMA((COPIES,)), pltpu.SemaphoreType.DMA((COPIES,)),
             pltpu.SemaphoreType.DMA((8, 2)), pltpu.SemaphoreType.DMA((8, 2)),
         ],

time: 68.7 us -> 66.7 us (0.971)
  Pallas kernels: 65.2 us -> 63.1 us
    pallas_call x1, Pallas kernels: 65.2 us -> 63.1 us  [per_device(): pl.pallas_call(kernel, out_shape=pltpu.VMEM((ROWS, 2048), BF), in_specs=[...]
where the time goes in v4:
time: 66.7 us; the launch traced here: 66.5 us
  Pallas kernels  63.1 us (95%)
  local copies, waits for them, and re-layouts  3.4 us (5%)
    pallas_call x1, Pallas kernels, per_device(): pl.pallas_call(kernel, out_shape=pltpu.VMEM((ROWS, 2048), BF), in_specs=[...  63.1 us
    unnamed x1, local copies, waits for them, and re-layouts  3.4 us

profile of v4, /device:TPU:1, one launch (start us, length us, event | category | flops | bytes accessed | tf_op | source)
XLA Modules:
  0.0 66.5 jit_solution(3114838906607931886)
XLA Ops:
  0.0 63.1 %galerkin.1 = bf16[2048,2048]{1,0:T(8,128)(2,1)S(1)} custom-call(s32[24,32]{1,0:T(8,128)} %bitcast.3, s32[12,2,32]{2,1,0:T(2,128)} %bitcast.4, s32[2,32]{1,0:T(2,128)} %bitcast.5, s32[2]{0:T(128)} %owners.1, bf16[32,2,64,64]{3,2,1,0:T(8,128)(2,1)} %p_hbm.1, bf16[32,24,64,64]{3,2,1,0:T(8,128)(2,1)} %l_hbm.1, bf16[32,2,12,64,64]{4,3,2,1,0:T(8,128)(2,1)} %s_hbm.1), custom_call_target="tpu_custom_call" | custom-call | tf_op jit(solution)/shard_map/galerkin/pallas_call | solution.py:418
  63.1 3.4 %copy.9 = bf16[2048,2048]{1,0:T(8,128)(2,1)} copy(bf16[2048,2048]{1,0:T(8,128)(2,1)S(1)} %galerkin.1) | data formatting | bytes 16777216

commit v5 on v4

--- a/solution.py
+++ b/solution.py
@@ -100,6 +100,25 @@
 
     def rows_at(base, index, size):
         return pl.ds(pl.multiple_of(base + index * size, size), size)
+
+    tile = jnp.full((RB, RB), K, jnp.int32)
+    for k in range(K):
+        tile = jnp.where(lcols[k : k + 1, :] == sub, k, tile)
+    vtable[0:RB, 0:RB] = tile
+    for s in range(2):
+        tile = jnp.full((RB, RB), K if s else KS, jnp.int32)
+        for k in range(KS):
+            tile = jnp.where(scols[k][s : s + 1, :] == sub, k, tile)
+        vtable[RB * (s + 1) : RB * (s + 2), 0:RB] = tile
+    to_scalar = pltpu.make_async_copy(vtable, table, load_sem.at[1])
+    to_scalar.start()
+
+    def clear(i, _):
+        aloc[i, K] = jnp.zeros((T, T), BF)
+        asec[i, KS] = jnp.zeros((T, T), BF)
+        return 0
+
+    lax.fori_loop(0, RB, clear, 0, unroll=4)
 
     load_p.wait()
 
@@ -197,25 +216,6 @@
         for copy in stage5[u]:
             copy.wait_recv()
 
-    tile = jnp.full((RB, RB), K, jnp.int32)
-    for k in range(K):
-        tile = jnp.where(lcols[k : k + 1, :] == sub, k, tile)
-    vtable[0:RB, 0:RB] = tile
-    for s in range(2):
-        tile = jnp.full((RB, RB), K if s else KS, jnp.int32)
-        for k in range(KS):
-            tile = jnp.where(scols[k][s : s + 1, :] == sub, k, tile)
-        vtable[RB * (s + 1) : RB * (s + 2), 0:RB] = tile
-    to_scalar = pltpu.make_async_copy(vtable, table, load_sem.at[1])
-    to_scalar.start()
-
-    def clear(i, _):
-        aloc[i, K] = jnp.zeros((T, T), BF)
-        asec[i, KS] = jnp.zeros((T, T), BF)
-        return 0
-
-    lax.fori_loop(0, RB, clear, 0, unroll=4)
-
     side_of = (lax.broadcasted_iota(jnp.int32, (16, 128), 1) >= T).astype(F32)
     slots = [(side_of + 2.0 * p).astype(BF) for p in range(4)]
 
@@ -301,10 +301,8 @@
 
     multiply(
         aloc, 0, range(16), pass1,
-        [(1, steps((step1, 0), (rest, 0))), (2, steps((step1, 1))), (3, steps((step2, 0)))],
+        [(1, steps((step1, 0))), (2, steps((step1, 1))), (3, steps((step2, 0), (step2, 2), (step2, 1), (step2, 3), (rest, 0)))],
     )
-    step2(1)
-
     def pass2(h):
         def use(m, ab):
             for n in range(2, 4):
@@ -324,14 +322,14 @@
         spread(h * 16, h * 16 + 16, lambda rows: pp[rows, :], lambda k: mpart[pl.ds(k, 1), :], d0, 1)
 
     begin(0)
-    multiply(aloc, 0, range(8), pass2(0), [(1, steps((step3, 0))), (3, steps((step3, 1), (step2, 2)))])
+    multiply(aloc, 0, range(8), pass2(0), [(1, steps((step3, 0), (step3, 1))), (3, steps((step3, 2), (step3, 3)))])
     step4(0)
-    step2(3)
+    step4(1)
     begin(1)
     multiply(
-        aloc, 0, range(8, 16), pass2(1), [(1, steps((step4, 1))), (3, steps((step3, 2)))]
+        aloc, 0, range(8, 16), pass2(1), [(2, steps((step4, 2)))]
     )
-    step3(3)
+    step4(3)
     load_s[1].start()
     load_s[0].wait()
 
@@ -370,11 +368,13 @@
         return use
 
     def last(m, ab):
-        for h in range(2):
-            cols = slice(h * HALF, (h + 1) * HALF)
+        for n in range(4):
+            cols = slice(n * 256, (n + 1) * 256)
+            start = (sides[n // 2] * 2 + core) * HALF + n % 2 * 256
             total = acc[rows_of(m), cols] + block(ab, ROWS, cols, d0, 0)
-            out[place(m, h)] = total.astype(BF)
-            result(m, h).start()
+            out[rows_of(m), pl.ds(pl.multiple_of(start, 256), 256)] = total.astype(BF)
+            if n % 2:
+                result(m, n // 2).start()
 
     def spread_all(u):
         s, half = UNITS[u]
@@ -386,8 +386,7 @@
 
     step5(0)
     spread_all(0)
-    multiply(asec, 1, range(8), pass3(0), [(2, steps((step5, 1), (step4, 2)))], ahead(1))
-    step4(3)
+    multiply(asec, 1, range(8), pass3(0), [(2, steps((step5, 1)))], ahead(1))
     multiply(asec, 1, range(8, 16), pass3(1), [(2, steps((step5, 2)))], ahead(2))
     load_s[1].wait()
     step5(3)

time: 66.7 us -> 64.7 us (0.970); the launches traced: 66.5 us -> 63.6 us
  Pallas kernels: 63.1 us -> 60.2 us
    pallas_call x1, Pallas kernels: 63.1 us -> 60.2 us  [per_device(): pl.pallas_call(kernel, out_shape=pltpu.VMEM((ROWS, 2048), BF), in_specs=[...]
where the time goes in v5:
time: 64.7 us; the launch traced here: 63.6 us
  Pallas kernels  60.2 us (93%)
  local copies, waits for them, and re-layouts  3.4 us (5%)
    pallas_call x1, Pallas kernels, per_device(): pl.pallas_call(kernel, out_shape=pltpu.VMEM((ROWS, 2048), BF), in_specs=[...  60.2 us
    unnamed x1, local copies, waits for them, and re-layouts  3.4 us

profile of v5, /device:TPU:1, one launch (start us, length us, event | category | flops | bytes accessed | tf_op | source)
XLA Modules:
  0.0 63.6 jit_solution(1199032713430345595)
XLA Ops:
  0.0 60.2 %galerkin.1 = bf16[2048,2048]{1,0:T(8,128)(2,1)S(1)} custom-call(s32[24,32]{1,0:T(8,128)} %bitcast.3, s32[12,2,32]{2,1,0:T(2,128)} %bitcast.4, s32[2,32]{1,0:T(2,128)} %bitcast.5, s32[2]{0:T(128)} %owners.1, bf16[32,2,64,64]{3,2,1,0:T(8,128)(2,1)} %p_hbm.1, bf16[32,24,64,64]{3,2,1,0:T(8,128)(2,1)} %l_hbm.1, bf16[32,2,12,64,64]{4,3,2,1,0:T(8,128)(2,1)} %s_hbm.1), custom_call_target="tpu_custom_call" | custom-call | tf_op jit(solution)/shard_map/galerkin/pallas_call | solution.py:417
  60.2 3.4 %copy.9 = bf16[2048,2048]{1,0:T(8,128)(2,1)} copy(bf16[2048,2048]{1,0:T(8,128)(2,1)S(1)} %galerkin.1) | data formatting | bytes 16777216
